TPU v7x, 512 devices: a whole 4x8x8 slice. The times are simulated.
512 devices in a mesh: row: 64 (over z, y_lo, core), rep: 8 (over x, y_hi).
Axes of the slice: x: 4, y: 8 (y_hi: 2, y_lo: 4; y = y_hi * 4 + y_lo), z: 8, core: 2. Of those that a mesh axis runs over, the one named last changes fastest.
Arguments:
- position: float32 [3, 262144], P(None, ('row', 'rep')), may hold values from -4 to 4
- velocity: float32 [3, 262144], P(None, ('row', 'rep')), may hold values from -3 to 3
- acceleration: float32 [3, 262144], P(None, ('row', 'rep')), may hold values from -12 to 12
- star_jerk: float32 [3, 262144], P(None, ('row', 'rep')), may hold values from -48 to 48
- star_mass: float32 [262144], P(('row', 'rep')), may hold values from 3.8146973e-06 to 6.1035156e-05
- time_last: float32 [262144], P(('row', 'rep')), may hold values from -0.25 to -0.05
- first_active: int32 [2048], replicated, may hold values from 0 to 262143, as said below
- second_active: int32 [2048], replicated, may hold values from 0 to 262143, as said below
Outputs:
- final_position: float32 [3, 262144], P(None, ('row', 'rep'))
- final_velocity: float32 [3, 262144], P(None, ('row', 'rep'))
- final_acceleration: float32 [3, 262144], P(None, ('row', 'rep'))
- final_jerk: float32 [3, 262144], P(None, ('row', 'rep'))
Inputs may be any that keep to these rules, and one draw needn't show every extreme that they name: `first_active`: 2048 distinct star indices; 0 and 262143 are always among them. `second_active`: 2048 distinct star indices; 0 and 262143 are always among them.
All inputs are finite; a program needn't handle non-finite values.
Results may differ from a plain program's by a relative error of at most 0.0003.
Values sent between devices are 32-bit elements; how exact they have to be, the bound alone decides.
A program may use at most 64 MiB of HBM per device.

v0:
```python
import jax
import jax.numpy as jnp
from jax import lax
from jax.sharding import PartitionSpec as P

EPS_SQ = 0.0004
STEP_TIMES = (0.0, 0.03125)


def predict(states, step_dt):
    posit = states[0:3]
    veloc = states[3:6]
    accel = states[6:9]
    change = states[9:12]
    pred_pos = posit + step_dt * (veloc + step_dt * (0.5 * accel + step_dt * change / 6.0))
    pred_vel = veloc + step_dt * (accel + step_dt * 0.5 * change)
    return (pred_pos, pred_vel)


def pair_terms(i_pos, i_vel, source):
    offset = source[0:3, None, :] - i_pos[:, :, None]
    relvel = source[3:6, None, :] - i_vel[:, :, None]
    dist_sq = jnp.sum(offset * offset, axis=0) + EPS_SQ
    inverse = lax.rsqrt(dist_sq)
    inv_sq = inverse * inverse
    weight = source[6][None, :] * inverse * inv_sq
    radial = jnp.sum(offset * relvel, axis=0) * inv_sq
    accel = jnp.sum(weight[None] * offset, axis=2)
    change = jnp.sum(weight[None] * (relvel - 3.0 * radial[None] * offset), axis=2)
    return (accel, change)


def sum_blocks(i_pos, i_vel, source, width):
    columns = source.shape[1]
    blocks = source.reshape(7, columns // width, width).transpose(1, 0, 2)

    def add_block(totals, block_data):
        accel, change = pair_terms(i_pos, i_vel, block_data)
        return ((totals[0] + accel, totals[1] + change), None)

    empty_sum = jnp.zeros(i_pos.shape, jnp.float32)
    totals, unused = lax.scan(add_block, (empty_sum, empty_sum), blocks)
    return totals


def correct(initial, accel_new, jerk_new, t_now):
    posit = initial[0:3]
    veloc = initial[3:6]
    accel = initial[6:9]
    change = initial[9:12]
    step_dt = t_now - initial[12]
    vel_new = (
        veloc + 0.5 * step_dt * (accel + accel_new) + step_dt * step_dt * (change - jerk_new) / 12.0
    )
    pos_new = (
        posit + 0.5 * step_dt * (veloc + vel_new) + step_dt * step_dt * (accel - accel_new) / 12.0
    )
    return jnp.concatenate([pos_new, vel_new, accel_new, jerk_new], axis=0)


def body(
    position, velocity, acceleration, star_jerk, star_mass, time_last, first_active, second_active
):
    rep_count = lax.axis_size("rep")
    row_index = lax.axis_index("row")
    rep_index = lax.axis_index("rep")
    local_count = position.shape[1]
    owned = (row_index * rep_count + rep_index) * local_count + lax.iota(jnp.int32, local_count)
    states = jnp.concatenate([position, velocity, acceleration, star_jerk], axis=0)
    time_now = time_last
    for t_now, active in ((STEP_TIMES[0], first_active), (STEP_TIMES[1], second_active)):
        match = (active[:, None] == owned[None, :]).astype(jnp.float32)
        held = jnp.concatenate([states, time_now[None]], axis=0)
        picked = jnp.einsum("cj,aj->ca", held, match, precision=lax.Precision.HIGHEST)
        initial = lax.psum_scatter(picked, "row", scatter_dimension=1, tiled=True)
        initial = lax.psum(initial, "rep")
        i_pos, i_vel = predict(initial[0:12], t_now - initial[12])
        pred_pos, pred_vel = predict(states, t_now - time_now)
        source = jnp.concatenate([pred_pos, pred_vel, star_mass[None]], axis=0)
        accel, change = sum_blocks(
            i_pos, i_vel, lax.all_gather(source, "row", axis=1, tiled=True), 1024
        )
        partial_terms = jnp.concatenate([accel, change], axis=0)
        total_terms = lax.psum(partial_terms, "rep")
        updated = correct(initial, total_terms[0:3], total_terms[3:6], t_now)
        arrived = lax.all_gather(updated, "row", axis=1, tiled=True)
        placed = jnp.einsum("ca,aj->cj", arrived, match, precision=lax.Precision.HIGHEST)
        was_hit = jnp.sum(match, axis=0) > 0.5
        states = jnp.where(was_hit[None], placed, states)
        time_now = jnp.where(was_hit, jnp.float32(t_now), time_now)
    return (states[0:3], states[3:6], states[6:9], states[9:12])


def solution(mesh):
    in_specs = (
        P(None, ("row", "rep")),
        P(None, ("row", "rep")),
        P(None, ("row", "rep")),
        P(None, ("row", "rep")),
        P(("row", "rep")),
        P(("row", "rep")),
        P(),
        P(),
    )
    out_specs = (
        P(None, ("row", "rep")),
        P(None, ("row", "rep")),
        P(None, ("row", "rep")),
        P(None, ("row", "rep")),
    )
    return jax.shard_map(body, mesh=mesh, in_specs=in_specs, out_specs=out_specs, check_vma=False)
```

profile of v0, /device:TPU:1, one launch (start us, length us, event | category | flops | bytes accessed | tf_op | source)
XLA Modules:
  0.0 889.7 jit_solution(4382447063566783991)
XLA Ops:
  7.2 2.3 concatenate.30
  9.6 3.6 fusion.23
  13.3 1.2 fusion.18
  14.7 91.5 %all_gather.12 = f32[7,32768]{1,0:T(8,128)S(1)} all-gather(f32[7,512]{1,0:T(8,128)S(1)} %pad_maximum_fusion.1), channel_id=1, replica_groups=mesh['row'=64,'rep'=8] {'row'}, dimensions={1}, use_global_device_ids=true | all-gather | bytes 931840 | tf_op jit(solution)/shard_map/all_gather | solution.py:81
  106.1 189.6 %reduce-scatter.7.cloned.1.call-done = f32[32,13]{1,0:T(8,128)} async-done(((f32[2048,13]{1,0:T(8,128)}), f32[32,13]{1,0:T(8,128)}) %reduce-scatter.7.cloned.1.call-update) | async-done | bytes 1680
  295.7 0.8 copy.27
  296.5 27.4 %psum.28 = f32[13,32]{1,0:T(8,128)S(1)} all-reduce(f32[13,32]{1,0:T(8,128)S(1)} %copy.27), channel_id=1, replica_groups=mesh['row'=64,'rep'=8] {'rep'}, use_global_device_ids=true, to_apply=%region_3.0 | all-reduce | flops 416 | bytes 3328 | tf_op jit(solution)/shard_map/psum | solution.py:76
  323.9 17.4 %while.26 = (s32[]{:T(128)}, f32[3,32]{1,0:T(4,128)S(1)}, f32[3,32]{1,0:T(4,128)S(1)}, f32[32,7,1024]{2,1,0:T(8,128)S(1)}, f32[3,32]{1,0:T(4,128)S(1)}, /*index=...) while((s32[]{:T(128)}, f32[3,32]{1,0:T(4,128)S(1)}, f32[3,32]{1,0:T(4,128)S(1)}, ...), condition=%wide.region_9.10_spmd.clone, body=%wide.region_4.9_spmd.clone.sunk | while | flops 1507525 | bytes 1163927 | solution.py:42
  324.2 0.3 fusion.55
  324.7 0.3 fusion.55
  325.3 0.3 fusion.55
  325.8 0.3 fusion.55
  326.4 0.3 fusion.55
  326.9 0.3 fusion.55
  327.5 0.3 fusion.55
  328.0 0.3 fusion.55
  330.2 0.3 fusion.55
  330.7 0.3 fusion.55
  331.3 0.3 fusion.55
  335.6 0.3 fusion.55
  336.1 0.3 fusion.55
  336.7 0.3 fusion.55
  340.5 0.3 fusion.55
  341.0 0.3 fusion.55
  341.3 20.4 %psum.29 = f32[6,32]{1,0:T(8,128)S(1)} all-reduce(f32[6,32]{1,0:T(8,128)S(1)} %pad_maximum_fusion.2), channel_id=1, replica_groups=mesh['row'=64,'rep'=8] {'rep'}, use_global_device_ids=true, to_apply=%region_10.11 | all-reduce | flops 192 | bytes 1536 | tf_op jit(solution)/shard_map/psum | solution.py:84
  361.8 88.1 %all-gather = f32[64,32,12]{1,2,0:T(8,128)S(1)} all-gather(f32[1,32,12]{1,2,0:T(8,128)S(1)} %maximum_bitcast_fusion), channel_id=1, replica_groups=mesh['row'=64,'rep'=8] {'row'}, dimensions={0}, use_global_device_ids=true | all-gather | bytes 99840 | tf_op jit(solution)/shard_map/all_gather | solution.py:86
  450.2 1.4 fusion.37
  451.5 2.9 fusion.20
  454.5 80.1 %all_gather.14 = f32[7,32768]{1,0:T(8,128)S(1)} all-gather(f32[7,512]{1,0:T(8,128)S(1)} %pad_maximum_fusion), channel_id=1, replica_groups=mesh['row'=64,'rep'=8] {'row'}, dimensions={1}, use_global_device_ids=true | all-gather | bytes 931840 | tf_op jit(solution)/shard_map/all_gather | solution.py:81
  534.6 191.7 %reduce-scatter.9.cloned.1.call-done = f32[32,13]{1,0:T(8,128)} async-done(((f32[2048,13]{1,0:T(8,128)}), f32[32,13]{1,0:T(8,128)}) %reduce-scatter.9.cloned.1.call-update) | async-done | bytes 1680
  726.3 0.8 copy.29
  727.1 27.5 %psum.30 = f32[13,32]{1,0:T(8,128)S(1)} all-reduce(f32[13,32]{1,0:T(8,128)S(1)} %copy.29), channel_id=1, replica_groups=mesh['row'=64,'rep'=8] {'rep'}, use_global_device_ids=true, to_apply=%region_12.13 | all-reduce | flops 416 | bytes 3328 | tf_op jit(solution)/shard_map/psum | solution.py:76
  754.6 17.4 %while.27 = (s32[]{:T(128)}, f32[3,32]{1,0:T(4,128)S(1)}, f32[3,32]{1,0:T(4,128)S(1)}, f32[32,7,1024]{2,1,0:T(8,128)S(1)}, f32[3,32]{1,0:T(4,128)S(1)}, /*index=...) while((s32[]{:T(128)}, f32[3,32]{1,0:T(4,128)S(1)}, f32[3,32]{1,0:T(4,128)S(1)}, ...), condition=%wide.region_18.19_spmd.clone, body=%wide.region_13.18_spmd.clone.sunk | while | flops 1507525 | bytes 1163927 | solution.py:42
  754.9 0.3 fusion.57
  755.4 0.3 fusion.57
  759.2 0.3 fusion.57
  759.8 0.3 fusion.57
  760.3 0.3 fusion.57
  764.7 0.3 fusion.57
  765.2 0.3 fusion.57
  765.7 0.3 fusion.57
  769.6 0.3 fusion.57
  770.1 0.3 fusion.57
  770.6 0.3 fusion.57
  772.0 20.4 %psum.31 = f32[6,32]{1,0:T(8,128)S(1)} all-reduce(f32[6,32]{1,0:T(8,128)S(1)} %pad_maximum_fusion.3), channel_id=1, replica_groups=mesh['row'=64,'rep'=8] {'rep'}, use_global_device_ids=true, to_apply=%region_19.20 | all-reduce | flops 192 | bytes 1536 | tf_op jit(solution)/shard_map/psum | solution.py:84
  792.4 88.1 %all-gather.1 = f32[64,32,12]{1,2,0:T(8,128)S(1)} all-gather(f32[1,32,12]{1,2,0:T(8,128)S(1)} %maximum_bitcast_fusion.1), channel_id=1, replica_groups=mesh['row'=64,'rep'=8] {'row'}, dimensions={0}, use_global_device_ids=true | all-gather | bytes 99840 | tf_op jit(solution)/shard_map/all_gather | solution.py:86
  880.9 1.3 fusion.34
  882.2 0.6 fusion.46
  (403 shorter events, 25.0 us)
Async XLA Ops:
  7.2 288.6 %reduce-scatter.7.cloned.1.call-start = ((), (), s32[]{:S(2)}) async-start(), calls=%async_computation.2 | async-start | bytes 1064960
  9.5 3.8 copy-start.6
  9.5 3.8 copy-start.7
  9.5 5.0 copy-start.4
  9.5 5.1 copy-start
  9.5 5.1 copy-start.1
  9.5 5.1 copy-start.2
  9.6 5.1 copy-start.3
  9.6 5.1 copy-start.5
  13.2 713.1 %reduce-scatter.9.cloned.1.call-start = ((), (), s32[]{:S(2)}) async-start(), calls=%async_computation.3 | async-start | bytes 1064960
Sparse Core Ops, SparseCore 0:
  13.3 282.3 reduce-scatter.6
  454.6 271.7 reduce-scatter.8
where the time goes:
time: 890 us
  blocking collectives  443 us (50%)
  waiting for transfers between devices  381 us (43%)
  other arithmetic  30.3 us (3%)
  between operations  14.3 us (2%)
  matrix products  9.18 us (1%)
    unnamed x4, waiting for transfers between devices  381 us
    all_gather x2, blocking collectives, body(): arrived = lax.all_gather(updated, 'row', axis=1, tiled=True)  176 us
    all_gather x2, blocking collectives, body(): lax.all_gather(source, 'row', axis=1, tiled=True)  172 us
    psum x2, blocking collectives, body(): initial = lax.psum(initial, 'rep')  54.8 us
    psum x2, blocking collectives, body(): total_terms = lax.psum(partial_terms, 'rep')  40.8 us
  transfers between devices with their start and end apart: 2, of which 2 were waited for; matrix products, arithmetic and copies ran while one was open for 0% of the time, Pallas kernels for 0%

commit v1 on v0

v1 whole, which is shorter than its diff:
```python
import functools

import jax
import jax.numpy as jnp
from jax import lax
from jax.experimental import pallas as pl
from jax.experimental.pallas import tpu as pltpu
from jax.sharding import PartitionSpec as P

MESH = pl.DeviceIdType.MESH
F32 = jnp.float32
BF16 = jnp.bfloat16
EPS_SQ = 0.0004
T_ONE = 0.0
T_TWO = 0.03125
ACT = 2048
OWN = 512
LANES = 128
SLICES = 16
BLOCKS = 32


def place():
    row, rep = lax.axis_index("row"), lax.axis_index("rep")
    slice_at = (row // 8) * 2 + row % 2
    block_at = (rep // 2) * 8 + (rep % 2) * 4 + (row // 2) % 4
    return slice_at, block_at


def device_of(slice_at, block_at):
    y = block_at % 8
    row = ((slice_at // 2) * 4 + y % 4) * 2 + slice_at % 2
    return row, (block_at // 8) * 2 + y // 4


def slice_peer(i, slice_at):
    half = (i + 1) // 2
    return (slice_at + 8 + half * (2 * (i % 2) - 1) + SLICES) % SLICES


def block_peer(i, block_at):
    j, k = i // 8, i % 8
    x_step = (1 - j // 2) * (2 + j) + (j // 2) * (3 - j)
    y_step = 4 + ((k + 1) // 2) * (2 * (k % 2) - 1)
    x = (block_at // 8 + x_step) % 4
    y = (block_at % 8 + y_step) % 8
    return x * 8 + y


def split_rows(rows):
    high = rows.astype(BF16).astype(F32)
    rest = rows - high
    middle = rest.astype(BF16).astype(F32)
    low = rest - middle
    return jnp.concatenate([high, middle, low, jnp.zeros_like(rows)], axis=0).astype(BF16)


def join_rows(parts):
    return parts[0:8] + (parts[8:16] + parts[16:24])


def pick(rows, match):
    return join_rows(jnp.dot(split_rows(rows), match, preferred_element_type=F32))


def put(rows, match):
    dims = (((1,), (1,)), ((), ()))
    return join_rows(lax.dot_general(split_rows(rows), match, dims, preferred_element_type=F32))


def predict(x, v, a, j, h):
    return (x + h * (v + h * (0.5 * a + h * j / 6.0)), v + h * (a + h * 0.5 * j))


def corrector_base(x, v, a, j, h):
    v_base = v + 0.5 * h * a + h * h * j / 12.0
    x_base = x + 0.5 * h * (v + v_base) + h * h * a / 12.0
    return x_base, v_base


def corrector_rest(x_base, v_base, a_new, j_new, h):
    v_new = v_base + 0.5 * h * a_new - h * h * j_new / 12.0
    x_new = x_base + (h * h / 6.0) * a_new - (h * h * h / 24.0) * j_new
    return x_new, v_new


def forces(i_rows, source, extra, i_wide, sums):
    columns = jnp.transpose(i_rows)
    for c in range(6):
        i_wide[c] = jnp.broadcast_to(columns[:, c : c + 1], (LANES, LANES))
    groups = 4

    def add_pairs(star, total, src):
        dx, dy, dz = src[0] - star[0], src[1] - star[1], src[2] - star[2]
        ux, uy, uz = src[3] - star[3], src[4] - star[4], src[5] - star[5]
        inverse = lax.rsqrt(dx * dx + dy * dy + (dz * dz + EPS_SQ))
        inv_sq = inverse * inverse
        weight = (src[6] * inverse) * inv_sq
        radial = (dx * ux + dy * uy + dz * uz) * inv_sq
        turn = weight * (3.0 * radial)
        return (
            total[0] + weight * dx,
            total[1] + weight * dy,
            total[2] + weight * dz,
            total[3] + (weight * ux - turn * dx),
            total[4] + (weight * uy - turn * dy),
            total[5] + (weight * uz - turn * dz),
        )

    def some_stars(g, _):
        base = pl.multiple_of(g * (8 * groups), 8 * groups)
        stars = [[i_wide[c, pl.ds(base + 8 * k, 8), :] for c in range(6)] for k in range(groups)]

        def some_sources(t, totals):
            lane = pl.multiple_of((t % 4) * LANES, LANES)
            src = [
                jnp.broadcast_to(source[t // 4, c : c + 1, pl.ds(lane, LANES)], (8, LANES))
                for c in range(7)
            ]
            return tuple(add_pairs(stars[k], totals[k], src) for k in range(groups))

        zero = jnp.zeros((8, LANES), F32)
        totals = lax.fori_loop(0, 64, some_sources, ((zero,) * 6,) * groups, unroll=4)
        if extra is not None:
            src = [jnp.broadcast_to(extra[c : c + 1, :], (8, LANES)) for c in range(7)]
            totals = tuple(add_pairs(stars[k], totals[k], src) for k in range(groups))
        for k in range(groups):
            for c in range(6):
                sums[c, pl.ds(base + 8 * k, 8), :] = totals[k][c]
        return 0

    lax.fori_loop(0, LANES // (8 * groups), some_stars, 0)
    lane = lax.broadcasted_iota(jnp.int32, (LANES, LANES), 1)
    columns = jnp.zeros((LANES, LANES), F32)
    for c in range(6):
        columns = jnp.where(lane == c, jnp.sum(sums[c], axis=1, keepdims=True), columns)
    return jnp.transpose(columns)[0:8]


def kernel(
    pos_ref, vel_ref, acc_ref, jerk_ref, mass_ref, time_ref, first_ref, second_ref,
    out_pos, out_vel, out_acc, out_jerk,
    match_one, match_two, match_both, rows_scr, i_wide, sums,
    pick_one, pick_two, base_mine,
    got_pick, got_base, src_one, src_two, all_pick, all_base,
    part_one, part_two, updated, total_one, total_two,
    send_sem, recv_sem,
):
    slice_at, block_at = place()

    barrier = pltpu.get_barrier_semaphore()

    def greet_block(i, _):
        to = device_of(slice_at, block_peer(i, block_at))
        pl.semaphore_signal(barrier, inc=1, device_id=to, device_id_type=MESH)
        return 0

    def greet_slice(i, _):
        to = device_of(slice_peer(i, slice_at), block_at)
        pl.semaphore_signal(barrier, inc=1, device_id=to, device_id_type=MESH)
        return 0

    lax.fori_loop(0, BLOCKS - 1, greet_block, 0)
    lax.fori_loop(0, SLICES - 1, greet_slice, 0)

    def to_slices(source_of, into, rows, sem):
        def one(i, _):
            peer = slice_peer(i, slice_at)
            pltpu.make_async_remote_copy(
                src_ref=source_of(peer).at[pl.ds(0, rows)],
                dst_ref=into.at[slice_at, pl.ds(0, rows)],
                send_sem=send_sem.at[sem],
                recv_sem=recv_sem.at[sem],
                device_id=device_of(peer, block_at),
                device_id_type=MESH,
            ).start()
            return 0

        lax.fori_loop(0, SLICES - 1, one, 0)

    def to_blocks(into, rows, sem):
        def one(i, _):
            mine = into.at[block_at, pl.ds(0, rows)]
            pltpu.make_async_remote_copy(
                src_ref=mine,
                dst_ref=mine,
                send_sem=send_sem.at[sem],
                recv_sem=recv_sem.at[sem],
                device_id=device_of(slice_at, block_peer(i, block_at)),
                device_id_type=MESH,
            ).start()
            return 0

        lax.fori_loop(0, BLOCKS - 1, one, 0)

    def wait(sems, buffer, rows, sem):
        whole = buffer.at[pl.ds(0, buffer.shape[0] - 1), pl.ds(0, rows)]
        pltpu.make_async_copy(whole, whole, sems.at[sem]).wait()

    pos, vel, acc, jerk = pos_ref[...], vel_ref[...], acc_ref[...], jerk_ref[...]
    time = jnp.concatenate([time_ref[k : k + 1, :] for k in range(4)], axis=1)
    mass = jnp.concatenate([mass_ref[k : k + 1, :] for k in range(4)], axis=1)
    base_id = (lax.axis_index("row") * 8 + lax.axis_index("rep")) * OWN
    owned = lax.broadcasted_iota(jnp.int32, (OWN, LANES), 0) + base_id

    def fill_match(match, ids):
        for q in range(SLICES):
            hit = jnp.broadcast_to(ids[q : q + 1, :], (OWN, LANES)) == owned
            match[:, q * LANES : (q + 1) * LANES] = jnp.where(hit, 1.0, 0.0).astype(BF16)

    fill_match(match_one, first_ref)
    h_one = T_ONE - time
    pred_pos, pred_vel = predict(pos, vel, acc, jerk, h_one)
    rows_scr[0:3, :] = pred_pos
    rows_scr[3:6, :] = pred_vel
    rows_scr[6:7, :] = mass
    rows_scr[7:8, :] = jnp.zeros_like(mass)
    rows = rows_scr[...]
    src_one[slice_at] = rows
    picked = pick(rows, match_one[...])
    for q in range(SLICES):
        pick_one[q] = picked[:, q * LANES : (q + 1) * LANES]
    got_pick[slice_at] = pick_one[slice_at]

    pl.semaphore_wait(barrier, SLICES + BLOCKS - 2)
    to_slices(lambda peer: pick_one.at[peer], got_pick, 6, 0)
    to_slices(lambda peer: src_one.at[slice_at], src_one, 8, 1)

    x_base, v_base = corrector_base(pos, vel, acc, jerk, h_one)
    rows_scr[0:3, :] = x_base
    rows_scr[3:6, :] = v_base
    rows_scr[6:7, :] = h_one
    rows_scr[7:8, :] = mass
    picked = pick(rows_scr[...], match_one[...])
    for q in range(SLICES):
        pick_two[q, 0:8, :] = picked[:, q * LANES : (q + 1) * LANES]
    fill_match(match_two, second_ref)
    pred_pos, pred_vel = predict(pos, vel, acc, jerk, T_TWO - time)
    rows_scr[0:3, :] = pred_pos
    rows_scr[3:6, :] = pred_vel
    rows_scr[6:7, :] = mass
    rows_scr[7:8, :] = jnp.zeros_like(mass)
    picked = pick(rows_scr[...], match_two[...])
    for q in range(SLICES):
        pick_two[q, 8:16, :] = picked[:, q * LANES : (q + 1) * LANES]
    got_base[slice_at] = pick_two[slice_at]
    ones = jnp.ones((16, ACT), BF16)
    dims = (((1,), (1,)), ((), ()))
    hit_one = lax.dot_general(ones, match_one[...], dims, preferred_element_type=F32)[0:1]
    hit_two = lax.dot_general(ones, match_two[...], dims, preferred_element_type=F32)[0:1]
    rows_scr[6:7, :] = jnp.where(hit_one > 0.5, 0.0, mass)
    src_two[slice_at] = rows_scr[...]

    wait(recv_sem, got_pick, 6, 0)
    total = got_pick[0]
    for q in range(1, SLICES):
        total = total + got_pick[q]
    all_pick[block_at] = total
    to_blocks(all_pick, 6, 2)
    to_slices(lambda peer: pick_two.at[peer], got_base, 16, 3)

    mine = jnp.broadcast_to(second_ref[pl.ds(slice_at, 1), :].astype(F32), (LANES, LANES))
    mine = jnp.transpose(mine)
    for q in range(SLICES):
        theirs = jnp.broadcast_to(first_ref[q : q + 1, :].astype(F32), (LANES, LANES))
        hit = jnp.where(mine == theirs, 1.0, 0.0).astype(BF16)
        match_both[:, q * LANES : (q + 1) * LANES] = hit

    wait(recv_sem, src_one, 8, 1)
    wait(recv_sem, all_pick, 6, 2)
    stars_one = all_pick[0]
    for s in range(1, BLOCKS):
        stars_one = stars_one + all_pick[s]

    wait(recv_sem, got_base, 16, 3)
    total = got_base[0]
    for q in range(1, SLICES):
        total = total + got_base[q]
    all_base[block_at] = total
    to_blocks(all_base, 16, 4)
    to_slices(lambda peer: src_two.at[slice_at], src_two, 8, 5)

    part_one[block_at] = forces(stars_one, src_one, None, i_wide, sums)
    to_blocks(part_one, 6, 6)

    wait(recv_sem, all_base, 16, 4)
    base = all_base[0]
    for s in range(1, BLOCKS):
        base = base + all_base[s]
    base_mine[...] = base
    wait(recv_sem, part_one, 6, 6)
    total = part_one[0]
    for s in range(1, BLOCKS):
        total = total + part_one[s]
    h = base_mine[6:7, :]
    a_new, j_new = total[0:3], total[3:6]
    x_new, v_new = corrector_rest(base_mine[0:3, :], base_mine[3:6, :], a_new, j_new, h)
    pred_pos, pred_vel = predict(x_new, v_new, a_new, j_new, T_TWO - T_ONE)
    updated[slice_at, 0:3, :] = pred_pos
    updated[slice_at, 3:6, :] = pred_vel
    updated[slice_at, 6:7, :] = base_mine[7:8, :]
    updated[slice_at, 7:8, :] = jnp.ones_like(h)
    to_slices(lambda peer: updated.at[slice_at], updated, 8, 7)
    total_one[slice_at] = total
    to_slices(lambda peer: total_one.at[slice_at], total_one, 6, 8)

    wait(recv_sem, src_two, 8, 5)
    wait(recv_sem, updated, 8, 7)
    moved = jnp.concatenate([updated[q] for q in range(SLICES)], axis=1)
    moved = put(moved, match_both[...])
    stars_two = jnp.where(moved[7:8] > 0.5, moved, base_mine[8:16, :])
    extra = updated[block_at // 2]
    lane = lax.broadcasted_iota(jnp.int32, (8, LANES), 1)
    row = lax.broadcasted_iota(jnp.int32, (8, LANES), 0)
    extra = jnp.where((row == 6) & (lane // 64 != block_at % 2), 0.0, extra)
    part_two[block_at] = forces(stars_two, src_two, extra, i_wide, sums)
    to_blocks(part_two, 6, 9)

    wait(recv_sem, total_one, 6, 8)
    placed = put(jnp.concatenate([total_one[q] for q in range(SLICES)], axis=1), match_one[...])
    was_hit = hit_one > 0.5
    a_new, j_new = placed[0:3], placed[3:6]
    x_new, v_new = corrector_rest(x_base, v_base, a_new, j_new, h_one)
    pos = jnp.where(was_hit, x_new, pos)
    vel = jnp.where(was_hit, v_new, vel)
    acc = jnp.where(was_hit, a_new, acc)
    jerk = jnp.where(was_hit, j_new, jerk)
    h_two = T_TWO - jnp.where(was_hit, T_ONE, time)
    x_base, v_base = corrector_base(pos, vel, acc, jerk, h_two)

    wait(recv_sem, part_two, 6, 9)
    total = part_two[0]
    for s in range(1, BLOCKS):
        total = total + part_two[s]
    total_two[slice_at] = total
    to_slices(lambda peer: total_two.at[slice_at], total_two, 6, 10)
    for sem, buffer, rows in (
        (0, got_pick, 6), (1, src_one, 8), (2, all_pick, 6), (3, got_base, 16), (4, all_base, 16), (5, src_two, 8),
        (6, part_one, 6), (7, updated, 8), (8, total_one, 6), (9, part_two, 6),
    ):
        wait(send_sem, buffer, rows, sem)
    wait(recv_sem, total_two, 6, 10)
    placed = put(jnp.concatenate([total_two[q] for q in range(SLICES)], axis=1), match_two[...])
    was_hit = hit_two > 0.5
    a_new, j_new = placed[0:3], placed[3:6]
    x_new, v_new = corrector_rest(x_base, v_base, a_new, j_new, h_two)
    out_pos[...] = jnp.where(was_hit, x_new, pos)
    out_vel[...] = jnp.where(was_hit, v_new, vel)
    out_acc[...] = jnp.where(was_hit, a_new, acc)
    out_jerk[...] = jnp.where(was_hit, j_new, jerk)
    wait(send_sem, total_two, 6, 10)


def body(position, velocity, acceleration, star_jerk, star_mass, time_last, first_active, second_active):
    vmem = pl.BlockSpec(memory_space=pltpu.VMEM)
    out = jax.ShapeDtypeStruct(position.shape, F32)
    slices = lambda rows, lanes=LANES: pltpu.VMEM((SLICES, rows, lanes), F32)
    blocks = lambda rows: pltpu.VMEM((BLOCKS, rows, LANES), F32)
    return pl.pallas_call(
        kernel,
        out_shape=(out,) * 4,
        in_specs=[vmem] * 8,
        out_specs=(vmem,) * 4,
        scratch_shapes=[
            pltpu.VMEM((OWN, ACT), BF16),
            pltpu.VMEM((OWN, ACT), BF16),
            pltpu.VMEM((LANES, ACT), BF16),
            pltpu.VMEM((8, OWN), F32),
            pltpu.VMEM((6, LANES, LANES), F32),
            pltpu.VMEM((6, LANES, LANES), F32),
            slices(8),
            slices(16),
            pltpu.VMEM((16, LANES), F32),
            slices(8),
            slices(16),
            slices(8, OWN),
            slices(8, OWN),
            blocks(8),
            blocks(16),
            blocks(8),
            blocks(8),
            slices(8),
            slices(8),
            slices(8),
            pltpu.SemaphoreType.DMA((11,)),
            pltpu.SemaphoreType.DMA((11,)),
        ],
        compiler_params=pltpu.CompilerParams(
            collective_id=0, has_side_effects=True, vmem_limit_bytes=40 * 1024 * 1024
        ),
    )(
        position,
        velocity,
        acceleration,
        star_jerk,
        star_mass.reshape(4, LANES),
        time_last.reshape(4, LANES),
        first_active.reshape(SLICES, LANES),
        second_active.reshape(SLICES, LANES),
    )


def solution(mesh):
    split = P(None, ("row", "rep"))
    flat = P(("row", "rep"))
    return jax.shard_map(
        body,
        mesh=mesh,
        in_specs=(split,) * 4 + (flat,) * 2 + (P(),) * 2,
        out_specs=(split,) * 4,
        check_vma=False,
    )
```

time: 890 us -> 78.2 us (0.09)
  blocking collectives: 443 us -> 0 us
  waiting for transfers between devices: 381 us -> 0 us
  Pallas kernels: 0 us -> 69.8 us
  other arithmetic: 30.3 us -> 0 us
  between operations: 14.3 us -> 0.67 us
  matrix products: 9.18 us -> 0 us
    unnamed x4 -> x0, waiting for transfers between devices: 381 us -> none
    all_gather x4 -> x0, blocking collectives: 348 us -> none  [the longest x2 176 us: body(): arrived = lax.all_gather(updated, 'row', axis=1, tiled=True)]
    psum x4 -> x0, blocking collectives: 95.6 us -> none  [the longest x2 54.8 us: body(): initial = lax.psum(initial, 'rep')]
    pallas_call x0 -> x1, Pallas kernels: none -> 69.8 us  [body(): pl.pallas_call(kernel, out_shape=(out,) * 4, in_specs=[vmem] * 8, out_spe...]
    reduce_sum x129 -> x0, other arithmetic: 26.3 us -> none  [the longest x64 16 us: pair_terms(): jnp.sum(weight[None] * (relvel - 3.0 * radial[None] * offset), axis=2)]
  transfers between devices with their start and end apart: 2 -> 0, of which waited for: 2 -> 0; matrix products, arithmetic and copies ran while one was open for 0% -> 0% of each run, Pallas kernels for 0% -> 0%
where the time goes in v1:
time: 78.2 us; the launch traced here: 77.7 us
  Pallas kernels  69.8 us (89%)
  local copies, waits for them, and re-layouts  7.25 us (9%)
    pallas_call x1, Pallas kernels, body(): pl.pallas_call(kernel, out_shape=(out,) * 4, in_specs=[vmem] * 8, out_spe...  69.8 us
    unnamed x20, local copies, waits for them, and re-layouts  7.25 us

profile of v1, /device:TPU:1, one launch (start us, length us, event | category | flops | bytes accessed | tf_op | source)
XLA Modules:
  0.0 77.7 jit_solution(3143886420039499723)
XLA Ops:
  0.6 0.0 copy-start.7
  0.6 0.0 copy-start.6
  0.7 0.7 copy-done.7
  1.3 0.0 copy-done.6
  1.3 0.0 copy-start
  1.3 0.7 copy-done
  2.0 0.0 copy-start.1
  2.0 0.7 copy-done.1
  2.7 0.0 copy-start.2
  2.7 0.7 copy-done.2
  3.4 0.0 copy-start.3
  3.4 0.7 copy-done.3
  4.1 0.0 copy-start.4
  4.1 0.7 copy-done.4
  4.8 0.0 copy-start.5
  4.8 0.7 copy-done.5
  5.5 69.8 %shard_map.111 = (f32[3,512]{1,0:T(4,128)S(1)}, f32[3,512]{1,0:T(4,128)S(1)}, f32[3,512]{1,0:T(4,128)S(1)}, f32[3,512]{1,0:T(4,128)S(1)}) custom-call(f32[3,512]{1,0:T(4,128)S(1)} %copy-done, f32[3,512]{1,0:T(4,128)S(1)} %copy-done.1, f32[3,512]{1,0:T(4,128)S(1)} %copy-done.2, f32[3,512]{1,0:T(4,128)S(1)} %copy-done.3, f32[4,128]{1,0:T(4,128)S(1)} %bitcast.6, ...), custom_call_target="tpu_custom_call" | custom-call | tf_op jit(solution)/shard_map/pallas_call | solution.py:359
  75.3 0.6 copy.16
  75.9 0.6 copy.17
  76.5 0.6 copy.18
  77.1 0.6 copy.19
Async XLA Ops:
  0.6 0.7 copy-start.7
  0.6 0.7 copy-start.6
  1.3 0.7 copy-start
  2.0 0.7 copy-start.1
  2.7 0.7 copy-start.2
  3.4 0.7 copy-start.3
  4.1 0.7 copy-start.4
  4.8 0.7 copy-start.5

commit v2 on v1

--- a/solution.py
+++ b/solution.py
@@ -27,24 +27,20 @@
     return slice_at, block_at
 
 
-def device_of(slice_at, block_at):
-    y = block_at % 8
-    row = ((slice_at // 2) * 4 + y % 4) * 2 + slice_at % 2
-    return row, (block_at // 8) * 2 + y // 4
-
-
-def slice_peer(i, slice_at):
-    half = (i + 1) // 2
-    return (slice_at + 8 + half * (2 * (i % 2) - 1) + SLICES) % SLICES
-
-
-def block_peer(i, block_at):
-    j, k = i // 8, i % 8
-    x_step = (1 - j // 2) * (2 + j) + (j // 2) * (3 - j)
-    y_step = 4 + ((k + 1) // 2) * (2 * (k % 2) - 1)
-    x = (block_at // 8 + x_step) % 4
-    y = (block_at % 8 + y_step) % 8
-    return x * 8 + y
+def peers(slice_at, block_at):
+    z, core = slice_at // 2, slice_at % 2
+    x, y = block_at // 8, block_at % 8
+    row = z * 8 + (y % 4) * 2 + core
+    rep = x * 2 + y // 4
+    near = (4, 3, 5, 2, 6, 1, 7, 0)
+    zs = [(z + k) % 8 for k in near]
+    ys = [(y + k) % 8 for k in near]
+    xs = [(x + k) % 4 for k in (2, 1, 3, 0)]
+    rows = [z * 8 + core + (k % 4) * 2 for k in ys]
+    reps = [k // 4 for k in ys]
+    others = [(k * 2 + side, (k * 8 + (y % 4) * 2 + side, rep)) for k in zs for side in (1 - core, core)]
+    blocks = [(xs[i] * 8 + ys[j], (rows[j], xs[i] * 2 + reps[j])) for i in range(4) for j in range(8)]
+    return others[:-1], blocks[:-1]
 
 
 def split_rows(rows):
@@ -138,65 +134,61 @@
 
 
 def kernel(
-    pos_ref, vel_ref, acc_ref, jerk_ref, mass_ref, time_ref, first_ref, second_ref,
+    pos_hbm, vel_hbm, acc_hbm, jerk_hbm, mass_hbm, time_hbm, first_hbm, second_hbm,
     out_pos, out_vel, out_acc, out_jerk,
     match_one, match_two, match_both, rows_scr, i_wide, sums,
     pick_one, pick_two, base_mine,
     got_pick, got_base, src_one, src_two, all_pick, all_base,
     part_one, part_two, updated, total_one, total_two,
-    send_sem, recv_sem,
+    pos_ref, vel_ref, acc_ref, jerk_ref, mass_ref, time_ref, first_ref, second_ref,
+    load_sem, send_sem, recv_sem,
 ):
     slice_at, block_at = place()
+    loads = [
+        pltpu.make_async_copy(source, into, load_sem.at[i])
+        for i, (source, into) in enumerate((
+            (first_hbm, first_ref), (pos_hbm, pos_ref), (vel_hbm, vel_ref), (acc_hbm, acc_ref), (jerk_hbm, jerk_ref),
+            (mass_hbm, mass_ref), (time_hbm, time_ref), (second_hbm, second_ref),
+        ))
+    ]
+    for load in loads:
+        load.start()
 
     barrier = pltpu.get_barrier_semaphore()
 
-    def greet_block(i, _):
-        to = device_of(slice_at, block_peer(i, block_at))
+    other_slices, other_blocks = peers(slice_at, block_at)
+    for _, to in other_blocks + other_slices:
         pl.semaphore_signal(barrier, inc=1, device_id=to, device_id_type=MESH)
-        return 0
-
-    def greet_slice(i, _):
-        to = device_of(slice_peer(i, slice_at), block_at)
-        pl.semaphore_signal(barrier, inc=1, device_id=to, device_id_type=MESH)
-        return 0
-
-    lax.fori_loop(0, BLOCKS - 1, greet_block, 0)
-    lax.fori_loop(0, SLICES - 1, greet_slice, 0)
 
     def to_slices(source_of, into, rows, sem):
-        def one(i, _):
-            peer = slice_peer(i, slice_at)
+        for peer, to in other_slices:
             pltpu.make_async_remote_copy(
                 src_ref=source_of(peer).at[pl.ds(0, rows)],
                 dst_ref=into.at[slice_at, pl.ds(0, rows)],
                 send_sem=send_sem.at[sem],
                 recv_sem=recv_sem.at[sem],
-                device_id=device_of(peer, block_at),
+                device_id=to,
                 device_id_type=MESH,
             ).start()
-            return 0
-
-        lax.fori_loop(0, SLICES - 1, one, 0)
 
     def to_blocks(into, rows, sem):
-        def one(i, _):
-            mine = into.at[block_at, pl.ds(0, rows)]
+        mine = into.at[block_at, pl.ds(0, rows)]
+        for _, to in other_blocks:
             pltpu.make_async_remote_copy(
                 src_ref=mine,
                 dst_ref=mine,
                 send_sem=send_sem.at[sem],
                 recv_sem=recv_sem.at[sem],
-                device_id=device_of(slice_at, block_peer(i, block_at)),
+                device_id=to,
                 device_id_type=MESH,
             ).start()
-            return 0
-
-        lax.fori_loop(0, BLOCKS - 1, one, 0)
 
     def wait(sems, buffer, rows, sem):
         whole = buffer.at[pl.ds(0, buffer.shape[0] - 1), pl.ds(0, rows)]
         pltpu.make_async_copy(whole, whole, sems.at[sem]).wait()
 
+    for load in loads:
+        load.wait()
     pos, vel, acc, jerk = pos_ref[...], vel_ref[...], acc_ref[...], jerk_ref[...]
     time = jnp.concatenate([time_ref[k : k + 1, :] for k in range(4)], axis=1)
     mass = jnp.concatenate([mass_ref[k : k + 1, :] for k in range(4)], axis=1)
@@ -351,15 +343,25 @@
     wait(send_sem, total_two, 6, 10)
 
 
+def write_out(pos, vel, acc, jerk, out_pos, out_vel, out_acc, out_jerk, sem):
+    pairs = ((pos, out_pos), (vel, out_vel), (acc, out_acc), (jerk, out_jerk))
+    copies = [pltpu.make_async_copy(a, b, sem.at[i]) for i, (a, b) in enumerate(pairs)]
+    for copy in copies:
+        copy.start()
+    for copy in copies:
+        copy.wait()
+
+
 def body(position, velocity, acceleration, star_jerk, star_mass, time_last, first_active, second_active):
     vmem = pl.BlockSpec(memory_space=pltpu.VMEM)
     out = jax.ShapeDtypeStruct(position.shape, F32)
+    held = pltpu.VMEM(position.shape, F32)
     slices = lambda rows, lanes=LANES: pltpu.VMEM((SLICES, rows, lanes), F32)
     blocks = lambda rows: pltpu.VMEM((BLOCKS, rows, LANES), F32)
-    return pl.pallas_call(
+    fields = pl.pallas_call(
         kernel,
-        out_shape=(out,) * 4,
-        in_specs=[vmem] * 8,
+        out_shape=(held,) * 4,
+        in_specs=[pl.BlockSpec(memory_space=pltpu.HBM)] * 8,
         out_specs=(vmem,) * 4,
         scratch_shapes=[
             pltpu.VMEM((OWN, ACT), BF16),
@@ -382,11 +384,15 @@
             slices(8),
             slices(8),
             slices(8),
+            *[pltpu.VMEM(position.shape, F32)] * 4,
+            *[pltpu.VMEM((4, LANES), F32)] * 2,
+            *[pltpu.VMEM((SLICES, LANES), jnp.int32)] * 2,
+            pltpu.SemaphoreType.DMA((8,)),
             pltpu.SemaphoreType.DMA((11,)),
             pltpu.SemaphoreType.DMA((11,)),
         ],
         compiler_params=pltpu.CompilerParams(
-            collective_id=0, has_side_effects=True, vmem_limit_bytes=40 * 1024 * 1024
+            collective_id=0, has_side_effects=True, vmem_limit_bytes=63 * 1024 * 1024
         ),
     )(
         position,
@@ -398,6 +404,13 @@
         first_active.reshape(SLICES, LANES),
         second_active.reshape(SLICES, LANES),
     )
+    return pl.pallas_call(
+        write_out,
+        out_shape=(out,) * 4,
+        in_specs=[vmem] * 4,
+        out_specs=(pl.BlockSpec(memory_space=pl.ANY),) * 4,
+        scratch_shapes=[pltpu.SemaphoreType.DMA((4,))],
+    )(*[pltpu.with_memory_space_constraint(f, pltpu.VMEM) for f in fields])
 
 
 def solution(mesh):

time: 78.2 us -> 68.4 us (0.87)
  local copies, waits for them, and re-layouts: 7.25 us -> 0 us
  Pallas kernels: 69.8 us -> 67.6 us
    unnamed x20 -> x0, local copies, waits for them, and re-layouts: 7.25 us -> none
    pallas_call x1 -> x2, Pallas kernels: 69.8 us -> 67.6 us  [the longest x1 66.9 us: body(): pl.pallas_call(kernel, out_shape=(held,) * 4, in_specs=[pl.BlockSpec(memo...]
where the time goes in v2:
time: 68.4 us; the launch traced here: 68.2 us
  Pallas kernels  67.6 us (99%)
    pallas_call x1, Pallas kernels, body(): pl.pallas_call(kernel, out_shape=(held,) * 4, in_specs=[pl.BlockSpec(memo...  66.9 us

profile of v2, /device:TPU:1, one launch (start us, length us, event | category | flops | bytes accessed | tf_op | source)
XLA Modules:
  0.0 68.2 jit_solution(1541175277846128699)
XLA Ops:
  0.6 66.9 %shard_map.111 = (f32[3,512]{1,0:T(4,128)S(1)}, f32[3,512]{1,0:T(4,128)S(1)}, f32[3,512]{1,0:T(4,128)S(1)}, f32[3,512]{1,0:T(4,128)S(1)}) custom-call(f32[3,512]{1,0:T(4,128)} %pos_hbm.1, f32[3,512]{1,0:T(4,128)} %vel_hbm.1, f32[3,512]{1,0:T(4,128)} %acc_hbm.1, f32[3,512]{1,0:T(4,128)} %jerk_hbm.1, f32[4,128]{1,0:T(4,128)} %bitcast.6, f32[4,128]{1,0:T(4,128)} %bitcast.7, ...), custom_call_target="tpu_custom_call" | custom-call | tf_op jit(solution)/shard_map/pallas_call | solution.py:361
  67.6 0.6 shard_map.112

commit v3 on v2

--- a/solution.py
+++ b/solution.py
@@ -116,7 +116,7 @@
             return tuple(add_pairs(stars[k], totals[k], src) for k in range(groups))
 
         zero = jnp.zeros((8, LANES), F32)
-        totals = lax.fori_loop(0, 64, some_sources, ((zero,) * 6,) * groups, unroll=4)
+        totals = lax.fori_loop(0, 64, some_sources, ((zero,) * 6,) * groups, unroll=16)
         if extra is not None:
             src = [jnp.broadcast_to(extra[c : c + 1, :], (8, LANES)) for c in range(7)]
             totals = tuple(add_pairs(stars[k], totals[k], src) for k in range(groups))
@@ -137,8 +137,8 @@
     pos_hbm, vel_hbm, acc_hbm, jerk_hbm, mass_hbm, time_hbm, first_hbm, second_hbm,
     out_pos, out_vel, out_acc, out_jerk,
     match_one, match_two, match_both, rows_scr, i_wide, sums,
-    pick_one, pick_two, base_mine,
-    got_pick, got_base, src_one, src_two, all_pick, all_base,
+    pick_one, pick_base, pick_two, base_mine,
+    got_pick, got_base, got_two, src_one, src_two, all_pick, all_base, all_two,
     part_one, part_two, updated, total_one, total_two,
     pos_ref, vel_ref, acc_ref, jerk_ref, mass_ref, time_ref, first_ref, second_ref,
     load_sem, send_sem, recv_sem,
@@ -157,6 +157,7 @@
     barrier = pltpu.get_barrier_semaphore()
 
     other_slices, other_blocks = peers(slice_at, block_at)
+
     for _, to in other_blocks + other_slices:
         pl.semaphore_signal(barrier, inc=1, device_id=to, device_id_type=MESH)
 
@@ -214,10 +215,6 @@
         pick_one[q] = picked[:, q * LANES : (q + 1) * LANES]
     got_pick[slice_at] = pick_one[slice_at]
 
-    pl.semaphore_wait(barrier, SLICES + BLOCKS - 2)
-    to_slices(lambda peer: pick_one.at[peer], got_pick, 6, 0)
-    to_slices(lambda peer: src_one.at[slice_at], src_one, 8, 1)
-
     x_base, v_base = corrector_base(pos, vel, acc, jerk, h_one)
     rows_scr[0:3, :] = x_base
     rows_scr[3:6, :] = v_base
@@ -225,7 +222,14 @@
     rows_scr[7:8, :] = mass
     picked = pick(rows_scr[...], match_one[...])
     for q in range(SLICES):
-        pick_two[q, 0:8, :] = picked[:, q * LANES : (q + 1) * LANES]
+        pick_base[q] = picked[:, q * LANES : (q + 1) * LANES]
+    got_base[slice_at] = pick_base[slice_at]
+
+    pl.semaphore_wait(barrier, SLICES + BLOCKS - 2)
+    to_slices(lambda peer: pick_one.at[peer], got_pick, 6, 0)
+    to_slices(lambda peer: pick_base.at[peer], got_base, 8, 3)
+    to_slices(lambda peer: src_one.at[slice_at], src_one, 8, 1)
+
     fill_match(match_two, second_ref)
     pred_pos, pred_vel = predict(pos, vel, acc, jerk, T_TWO - time)
     rows_scr[0:3, :] = pred_pos
@@ -234,8 +238,9 @@
     rows_scr[7:8, :] = jnp.zeros_like(mass)
     picked = pick(rows_scr[...], match_two[...])
     for q in range(SLICES):
-        pick_two[q, 8:16, :] = picked[:, q * LANES : (q + 1) * LANES]
-    got_base[slice_at] = pick_two[slice_at]
+        pick_two[q] = picked[:, q * LANES : (q + 1) * LANES]
+    got_two[slice_at] = pick_two[slice_at]
+    to_slices(lambda peer: pick_two.at[peer], got_two, 6, 11)
     ones = jnp.ones((16, ACT), BF16)
     dims = (((1,), (1,)), ((), ()))
     hit_one = lax.dot_general(ones, match_one[...], dims, preferred_element_type=F32)[0:1]
@@ -249,7 +254,6 @@
         total = total + got_pick[q]
     all_pick[block_at] = total
     to_blocks(all_pick, 6, 2)
-    to_slices(lambda peer: pick_two.at[peer], got_base, 16, 3)
 
     mine = jnp.broadcast_to(second_ref[pl.ds(slice_at, 1), :].astype(F32), (LANES, LANES))
     mine = jnp.transpose(mine)
@@ -258,24 +262,29 @@
         hit = jnp.where(mine == theirs, 1.0, 0.0).astype(BF16)
         match_both[:, q * LANES : (q + 1) * LANES] = hit
 
+    wait(recv_sem, got_base, 8, 3)
+    total = got_base[0]
+    for q in range(1, SLICES):
+        total = total + got_base[q]
+    all_base[block_at] = total
+    to_blocks(all_base, 8, 4)
+
     wait(recv_sem, src_one, 8, 1)
     wait(recv_sem, all_pick, 6, 2)
     stars_one = all_pick[0]
     for s in range(1, BLOCKS):
         stars_one = stars_one + all_pick[s]
-
-    wait(recv_sem, got_base, 16, 3)
-    total = got_base[0]
-    for q in range(1, SLICES):
-        total = total + got_base[q]
-    all_base[block_at] = total
-    to_blocks(all_base, 16, 4)
-    to_slices(lambda peer: src_two.at[slice_at], src_two, 8, 5)
-
     part_one[block_at] = forces(stars_one, src_one, None, i_wide, sums)
     to_blocks(part_one, 6, 6)
-
-    wait(recv_sem, all_base, 16, 4)
+    wait(recv_sem, got_two, 6, 11)
+    total = got_two[0]
+    for q in range(1, SLICES):
+        total = total + got_two[q]
+    all_two[block_at] = total
+    to_blocks(all_two, 6, 12)
+    to_slices(lambda peer: src_two.at[slice_at], src_two, 8, 5)
+
+    wait(recv_sem, all_base, 8, 4)
     base = all_base[0]
     for s in range(1, BLOCKS):
         base = base + all_base[s]
@@ -296,11 +305,15 @@
     total_one[slice_at] = total
     to_slices(lambda peer: total_one.at[slice_at], total_one, 6, 8)
 
+    wait(recv_sem, all_two, 6, 12)
+    stars_two = all_two[0]
+    for s in range(1, BLOCKS):
+        stars_two = stars_two + all_two[s]
     wait(recv_sem, src_two, 8, 5)
     wait(recv_sem, updated, 8, 7)
     moved = jnp.concatenate([updated[q] for q in range(SLICES)], axis=1)
     moved = put(moved, match_both[...])
-    stars_two = jnp.where(moved[7:8] > 0.5, moved, base_mine[8:16, :])
+    stars_two = jnp.where(moved[7:8] > 0.5, moved, stars_two)
     extra = updated[block_at // 2]
     lane = lax.broadcasted_iota(jnp.int32, (8, LANES), 1)
     row = lax.broadcasted_iota(jnp.int32, (8, LANES), 0)
@@ -327,8 +340,9 @@
     total_two[slice_at] = total
     to_slices(lambda peer: total_two.at[slice_at], total_two, 6, 10)
     for sem, buffer, rows in (
-        (0, got_pick, 6), (1, src_one, 8), (2, all_pick, 6), (3, got_base, 16), (4, all_base, 16), (5, src_two, 8),
+        (0, got_pick, 6), (1, src_one, 8), (2, all_pick, 6), (3, got_base, 8), (4, all_base, 8), (5, src_two, 8),
         (6, part_one, 6), (7, updated, 8), (8, total_one, 6), (9, part_two, 6),
+        (11, got_two, 6), (12, all_two, 6),
     ):
         wait(send_sem, buffer, rows, sem)
     wait(recv_sem, total_two, 6, 10)
@@ -371,14 +385,17 @@
             pltpu.VMEM((6, LANES, LANES), F32),
             pltpu.VMEM((6, LANES, LANES), F32),
             slices(8),
-            slices(16),
-            pltpu.VMEM((16, LANES), F32),
-            slices(8),
-            slices(16),
+            slices(8),
+            slices(8),
+            pltpu.VMEM((8, LANES), F32),
+            slices(8),
+            slices(8),
+            slices(8),
             slices(8, OWN),
             slices(8, OWN),
             blocks(8),
-            blocks(16),
+            blocks(8),
+            blocks(8),
             blocks(8),
             blocks(8),
             slices(8),
@@ -388,8 +405,8 @@
             *[pltpu.VMEM((4, LANES), F32)] * 2,
             *[pltpu.VMEM((SLICES, LANES), jnp.int32)] * 2,
             pltpu.SemaphoreType.DMA((8,)),
-            pltpu.SemaphoreType.DMA((11,)),
-            pltpu.SemaphoreType.DMA((11,)),
+            pltpu.SemaphoreType.DMA((13,)),
+            pltpu.SemaphoreType.DMA((13,)),
         ],
         compiler_params=pltpu.CompilerParams(
             collective_id=0, has_side_effects=True, vmem_limit_bytes=63 * 1024 * 1024

time: 68.4 us -> 66.1 us (0.966)
  Pallas kernels: 67.6 us -> 65.3 us
    pallas_call x1, Pallas kernels: 66.9 us -> 64.6 us  [body(): pl.pallas_call(kernel, out_shape=(held,) * 4, in_specs=[pl.BlockSpec(memo...]
where the time goes in v3:
time: 66.1 us; the launch traced here: 65.9 us
  Pallas kernels  65.3 us (99%)
    pallas_call x1, Pallas kernels, body(): pl.pallas_call(kernel, out_shape=(held,) * 4, in_specs=[pl.BlockSpec(memo...  64.6 us

profile of v3, /device:TPU:1, one launch (start us, length us, event | category | flops | bytes accessed | tf_op | source)
XLA Modules:
  0.0 65.9 jit_solution(14941084520340618709)
XLA Ops:
  0.6 64.6 %shard_map.111 = (f32[3,512]{1,0:T(4,128)S(1)}, f32[3,512]{1,0:T(4,128)S(1)}, f32[3,512]{1,0:T(4,128)S(1)}, f32[3,512]{1,0:T(4,128)S(1)}) custom-call(f32[3,512]{1,0:T(4,128)} %pos_hbm.1, f32[3,512]{1,0:T(4,128)} %vel_hbm.1, f32[3,512]{1,0:T(4,128)} %acc_hbm.1, f32[3,512]{1,0:T(4,128)} %jerk_hbm.1, f32[4,128]{1,0:T(4,128)} %bitcast.6, f32[4,128]{1,0:T(4,128)} %bitcast.7, ...), custom_call_target="tpu_custom_call" | custom-call | tf_op jit(solution)/shard_map/pallas_call | solution.py:375
  65.2 0.6 shard_map.112

commit v4 on v3

--- a/solution.py
+++ b/solution.py
@@ -39,7 +39,7 @@
     rows = [z * 8 + core + (k % 4) * 2 for k in ys]
     reps = [k // 4 for k in ys]
     others = [(k * 2 + side, (k * 8 + (y % 4) * 2 + side, rep)) for k in zs for side in (1 - core, core)]
-    blocks = [(xs[i] * 8 + ys[j], (rows[j], xs[i] * 2 + reps[j])) for i in range(4) for j in range(8)]
+    blocks = [(xs[i] * 8 + ys[j], (rows[j], xs[i] * 2 + reps[j])) for j in range(8) for i in range(4)]
     return others[:-1], blocks[:-1]
 
 
@@ -92,15 +92,14 @@
         inverse = lax.rsqrt(dx * dx + dy * dy + (dz * dz + EPS_SQ))
         inv_sq = inverse * inverse
         weight = (src[6] * inverse) * inv_sq
-        radial = (dx * ux + dy * uy + dz * uz) * inv_sq
-        turn = weight * (3.0 * radial)
+        radial = (dx * ux + dy * uy + dz * uz) * (3.0 * inv_sq)
         return (
             total[0] + weight * dx,
             total[1] + weight * dy,
             total[2] + weight * dz,
-            total[3] + (weight * ux - turn * dx),
-            total[4] + (weight * uy - turn * dy),
-            total[5] + (weight * uz - turn * dz),
+            total[3] + weight * (ux - radial * dx),
+            total[4] + weight * (uy - radial * dy),
+            total[5] + weight * (uz - radial * dz),
         )
 
     def some_stars(g, _):
@@ -151,14 +150,15 @@
             (mass_hbm, mass_ref), (time_hbm, time_ref), (second_hbm, second_ref),
         ))
     ]
+    barrier = pltpu.get_barrier_semaphore()
+
+    other_slices, other_blocks = peers(slice_at, block_at)
+
+    for _, to in other_blocks:
+        pl.semaphore_signal(barrier, inc=1, device_id=to, device_id_type=MESH)
     for load in loads:
         load.start()
-
-    barrier = pltpu.get_barrier_semaphore()
-
-    other_slices, other_blocks = peers(slice_at, block_at)
-
-    for _, to in other_blocks + other_slices:
+    for _, to in other_slices:
         pl.semaphore_signal(barrier, inc=1, device_id=to, device_id_type=MESH)
 
     def to_slices(source_of, into, rows, sem):
@@ -303,7 +303,6 @@
     updated[slice_at, 7:8, :] = jnp.ones_like(h)
     to_slices(lambda peer: updated.at[slice_at], updated, 8, 7)
     total_one[slice_at] = total
-    to_slices(lambda peer: total_one.at[slice_at], total_one, 6, 8)
 
     wait(recv_sem, all_two, 6, 12)
     stars_two = all_two[0]
@@ -320,6 +319,7 @@
     extra = jnp.where((row == 6) & (lane // 64 != block_at % 2), 0.0, extra)
     part_two[block_at] = forces(stars_two, src_two, extra, i_wide, sums)
     to_blocks(part_two, 6, 9)
+    to_slices(lambda peer: total_one.at[slice_at], total_one, 6, 8)
 
     wait(recv_sem, total_one, 6, 8)
     placed = put(jnp.concatenate([total_one[q] for q in range(SLICES)], axis=1), match_one[...])

time: 66.1 us -> 64.8 us (0.980)
  Pallas kernels: 65.3 us -> 64 us
    pallas_call x1, Pallas kernels: 64.6 us -> 63.4 us  [body(): pl.pallas_call(kernel, out_shape=(held,) * 4, in_specs=[pl.BlockSpec(memo...]
where the time goes in v4:
time: 64.8 us; the launch traced here: 64.7 us
  Pallas kernels  64 us (99%)
    pallas_call x1, Pallas kernels, body(): pl.pallas_call(kernel, out_shape=(held,) * 4, in_specs=[pl.BlockSpec(memo...  63.4 us

profile of v4, /device:TPU:1, one launch (start us, length us, event | category | flops | bytes accessed | tf_op | source)
XLA Modules:
  0.0 64.7 jit_solution(14368534082596581414)
XLA Ops:
  0.6 63.4 %shard_map.111 = (f32[3,512]{1,0:T(4,128)S(1)}, f32[3,512]{1,0:T(4,128)S(1)}, f32[3,512]{1,0:T(4,128)S(1)}, f32[3,512]{1,0:T(4,128)S(1)}) custom-call(f32[3,512]{1,0:T(4,128)} %pos_hbm.1, f32[3,512]{1,0:T(4,128)} %vel_hbm.1, f32[3,512]{1,0:T(4,128)} %acc_hbm.1, f32[3,512]{1,0:T(4,128)} %jerk_hbm.1, f32[4,128]{1,0:T(4,128)} %bitcast.6, f32[4,128]{1,0:T(4,128)} %bitcast.7, ...), custom_call_target="tpu_custom_call" | custom-call | tf_op jit(solution)/shard_map/pallas_call | solution.py:375
  64.0 0.6 %shard_map.112 = (f32[3,512]{1,0:T(4,128)}, f32[3,512]{1,0:T(4,128)}, f32[3,512]{1,0:T(4,128)}, f32[3,512]{1,0:T(4,128)}) custom-call(f32[3,512]{1,0:T(4,128)S(1)} %get-tuple-element.8.pos, f32[3,512]{1,0:T(4,128)S(1)} %get-tuple-element.9.vel, f32[3,512]{1,0:T(4,128)S(1)} %get-tuple-element.10.acc, f32[3,512]{1,0:T(4,128)S(1)} %get-tuple-element.11.jerk), custom_call_target="tpu_custom_call" | custom-call | tf_op jit(solution)/shard_map/pallas_call | solution.py:424
